TPU v7x, 32 devices: a whole 2x2x4 slice. The times are simulated.
32 devices in a mesh: group: 4 (over z), member: 8 (over y, x, core).
Axes of the slice: x: 2, y: 2, z: 4, core: 2. Of those that a mesh axis runs over, the one named last changes fastest.
Arguments:
- diag_tiles: bfloat16 [512, 4, 128, 128], P(('group', 'member')), may hold values from -0.21875 to 0.21875
- diag_cols: int32 [512, 4], P(('group', 'member')), may hold values from 0 to 15
- offd_tiles: bfloat16 [512, 2, 128, 128], P(('group', 'member')), may hold values from -0.21875 to 0.21875
- offd_cols: int32 [512, 2], P(('group', 'member')), may hold values from 0 to 7, as said below
- offd_count: int32 [512], P(('group', 'member')), may hold values from 0 to 2
- p_tiles: bfloat16 [512, 2, 128, 128], P(('group', 'member')), may hold values from -2 to 2
- p_cols: int32 [512, 2], P(('group', 'member')), may hold values from 0 to 31, as said below
- send_rows: int32 [32, 8, 1], P(('group', 'member')), may hold values from 0 to 15
- coarse_cols: int32 [32, 8], replicated, may hold values from 0 to 31, as said below
Outputs:
- coarse_tiles: float32 [32, 8, 128, 128], P(('group', 'member'))
Inputs may be any that keep to these rules, and one draw needn't show every extreme that they name: `p_cols`: the 2 entries of fine block row f on group g and member m are distinct coarse rows h * 8 + m with h one of g, (g + 1) % 4, (g + 2) % 4. `offd_cols`: A remote tile of a fine block row on member m reads a row sent by member (m - 1) % 8, (m + 1) % 8 or (m + 4) % 8. `coarse_cols`: the 8 entries of coarse row h * 8 + m are distinct; they are that row itself and the rows ((h + 1) % 4) * 8 + m, ((h - 1) % 4) * 8 + m, ((h + 2) % 4) * 8 + m, then four rows h2 * 8 + m2 with h2 among h - 1, h, h + 1, h + 2 and m2 among m - 1, m + 1, m + 8 // 2 (both modulo their counts).
All inputs are finite; a program needn't handle non-finite values.
Results may differ from a plain program's by a relative error of at most 0.005.
Values may be sent and summed in bfloat16 or wider, within the bound.
A program may use at most 128 MiB of HBM per device.

v0:
```python
import jax
import jax.numpy as jnp
from jax import lax
from jax.sharding import PartitionSpec as P


def product_terms(a_tiles, p_rows, p_ids, targets, live):
    ap_tiles = jnp.einsum(
        "rkab,rkqbc->rkqac", a_tiles, p_rows, preferred_element_type=jnp.float32
    ).astype(jnp.bfloat16)
    match = p_ids[:, None, None, :, :] == targets[:, :, :, None, None]
    match = jnp.logical_and(match, live[:, None, None, :, None])
    return jnp.einsum(
        "rpskq,rkqac->rpsac",
        match.astype(jnp.bfloat16),
        ap_tiles,
        preferred_element_type=jnp.float32,
    )


def on_device(
    diag_tiles,
    diag_cols,
    offd_tiles,
    offd_cols,
    offd_count,
    p_tiles,
    p_cols,
    send_rows,
    coarse_cols,
):
    rows = p_tiles.shape[0]
    width = p_tiles.shape[-1]
    groups = lax.axis_size("group")
    members = lax.axis_size("member")
    coarse_total = coarse_cols.shape[0]
    picked = send_rows[0]
    out_tiles = p_tiles[picked]
    out_cols = p_cols[picked]
    recv_tiles, recv_cols = (
        lax.all_to_all(out_tiles, "member", split_axis=0, concat_axis=0, tiled=True),
        lax.all_to_all(out_cols, "member", split_axis=0, concat_axis=0, tiled=True),
    )
    flat_tiles = recv_tiles.reshape((-1,) + p_tiles.shape[1:])
    flat_cols = recv_cols.reshape(-1, p_cols.shape[1])
    flat_tiles, flat_cols, diag_tiles, diag_cols = lax.optimization_barrier(
        (flat_tiles, flat_cols, diag_tiles, diag_cols)
    )
    lookup = (p_cols[:, :, None] == jnp.arange(coarse_total)[None, None, :]).astype(jnp.float32)
    targets = jnp.einsum(
        "rpc,ck->rpk", lookup, coarse_cols.astype(jnp.float32), precision=lax.Precision.HIGHEST
    ).astype(jnp.int32)
    full_live = jnp.ones(diag_cols.shape, dtype=bool)
    summed = product_terms(diag_tiles, p_tiles[diag_cols], p_cols[diag_cols], targets, full_live)
    counted = jnp.arange(offd_cols.shape[1])[None, :] < offd_count[:, None]
    summed = summed + product_terms(
        offd_tiles, flat_tiles[offd_cols], flat_cols[offd_cols], targets, counted
    )
    y_tiles = summed.astype(jnp.bfloat16)
    route = (jnp.arange(groups)[None, :, None] == (p_cols // members)[:, None, :]).astype(
        jnp.float32
    )
    block = 8
    blocks = rows // block
    kept = y_tiles.shape[2]
    p_blocks = p_tiles.reshape((blocks, block) + p_tiles.shape[1:])
    y_blocks = y_tiles.reshape((blocks, block) + y_tiles.shape[1:])
    r_blocks = route.reshape((blocks, block) + route.shape[1:])

    def accumulate(carry, pieces):
        p_part, y_part, r_part = pieces
        products = jnp.einsum(
            "rpba,rpsbc->rpsac", p_part, y_part, preferred_element_type=jnp.float32
        )
        added = jnp.einsum("rgp,rpsac->gsac", r_part, products, precision=lax.Precision.HIGHEST)
        return (carry + added, None)

    start = jnp.zeros((groups, kept, width, width), jnp.float32)
    partial_rows, _ = lax.scan(accumulate, start, (p_blocks, y_blocks, r_blocks))
    rounded = partial_rows.astype(jnp.bfloat16)
    arrived = lax.all_to_all(rounded, "group", split_axis=0, concat_axis=0, tiled=True)
    return jnp.sum(arrived.astype(jnp.float32), axis=0, keepdims=True)


def solution(mesh):
    return jax.shard_map(
        on_device,
        mesh=mesh,
        in_specs=(
            P(("group", "member"), None, None, None),
            P(("group", "member"), None),
            P(("group", "member"), None, None, None),
            P(("group", "member"), None),
            P(("group", "member")),
            P(("group", "member"), None, None, None),
            P(("group", "member"), None),
            P(("group", "member"), None, None),
            P(),
        ),
        out_specs=P(("group", "member"), None, None, None),
        check_vma=False,
    )
```

profile of v0, /device:TPU:0, one launch (start us, length us, event | category | flops | bytes accessed | tf_op | source)
XLA Modules:
  0.0 171.2 jit_solution(262946125327156658)
XLA Ops:
  0.0 0.0 copy-start
  0.0 0.0 copy-start.2
  0.0 0.9 copy.45
  0.9 0.7 fusion.29
  1.6 1.1 gather_fusion.1
  2.8 5.2 %all-to-all-start.1 = ((s32[8,1,2]{2,1,0:T(1,128)}), s32[8,1,2]{2,1,0:T(1,128)S(1)}, u32[]{:S(2)}, u32[]{:S(2)}) async-start(s32[8,1,2]{2,1,0:T(1,128)} %bitcast.40), calls=%async_computation.1 | async-start | bytes 8192 | tf_op jit(solution)/shard_map/all_to_all | solution.py:42
  7.9 0.7 and_select_fusion
  8.6 2.6 %gather_fusion = bf16[8,2,128,128]{3,2,1,0:T(8,128)(2,1)} fusion(bf16[16,2,128,128]{3,2,1,0:T(8,128)(2,1)} %param.16, s32[1024]{0:T(1024)S(1)} %pad_clamp_fusion.2), kind=kCustom, calls=%fused_computation | custom fusion | bytes 1048608 | tf_op jit(solution)/shard_map/gather | solution.py:38
  11.3 0.9 convolution_convert_fusion
  12.2 0.8 compare_select_fusion.1
  12.9 0.1 copy.51
  13.0 0.1 reshape.117
  13.1 0.0 all-to-all-done.1
  13.1 4.2 %all-to-all-start = ((bf16[8,1,2,128,128]{4,3,2,1,0:T(8,128)(2,1)}), bf16[8,1,2,128,128]{4,3,2,1,0:T(8,128)(2,1)}, u32[]{:S(2)}, u32[]{:S(2)}) async-start(bf16[8,1,2,128,128]{4,3,2,1,0:T(8,128)(2,1)} %bitcast.102), calls=%async_computation | async-start | bytes 1048576 | tf_op jit(solution)/shard_map/all_to_all | solution.py:41
  17.3 0.1 copy.48
  17.4 0.1 eq.56
  17.5 0.7 iota_compare_fusion.2
  18.2 0.1 copy.43
  18.3 8.8 %all-to-all-done = bf16[8,1,2,128,128]{4,3,2,1,0:T(8,128)(2,1)} async-done(((bf16[8,1,2,128,128]{4,3,2,1,0:T(8,128)(2,1)}), bf16[8,1,2,128,128]{4,3,2,1,0:T(8,128)(2,1)}, u32[]{:S(2)}, u32[]{:S(2)}) %all-to-all-start) | async-done | bytes 524320 | tf_op jit(solution)/shard_map/all_to_all | solution.py:41
  27.2 0.7 compare_select_fusion
  27.8 0.1 copy.44
  27.9 0.1 reshape.101
  28.0 0.0 copy-done.2
  28.0 3.0 %gather_fusion.3 = bf16[64,2,128,128]{3,2,1,0:T(8,128)(2,1)} fusion(bf16[16,2,128,128]{3,2,1,0:T(8,128)(2,1)S(1)} %copy-done.2, s32[1024]{0:T(1024)S(1)} %pad_clamp_fusion.1), kind=kCustom, calls=%fused_computation.3 | custom fusion | bytes 8388864 | tf_op jit(solution)/shard_map/gather | solution.py:54
  31.1 0.6 gather_fusion.2
  31.7 0.0 copy-done
  31.7 5.5 %convert_bitcast_fusion = bf16[16,4,2,128,128,1]{3,4,2,1,0,5:T(8,128)(2,1)} fusion(bf16[16,4,2,128,128]{4,3,2,1,0:T(8,128)(2,1)} %bitcast.100, bf16[16,4,128,128]{3,2,1,0:T(8,128)(2,1)S(1)} %copy-done), kind=kOutput, calls=%fused_computation.19 | convolution fusion | flops 538968064 | bytes 10485760 | tf_op jit(solution)/shard_map/rkab,rkqbc->rkqac/dot_general | solution.py:8
  37.1 7.4 %copy.66 = bf16[16,4,2,128,128,1]{4,1,2,3,5,0:T(4,128)(2,1)} copy(bf16[16,4,2,128,128,1]{3,4,2,1,0,5:T(8,128)(2,1)} %convert_bitcast_fusion) | data formatting | bytes 8388608 | tf_op jit(solution)/shard_map/convert_element_type | solution.py:10
  44.6 0.2 copy.47
  44.8 2.0 %gather_fusion.5 = bf16[32,2,128,128]{3,2,1,0:T(8,128)(2,1)S(1)} fusion(bf16[8,2,128,128]{3,2,1,0:T(8,128)(2,1)} %bitcast.3, s32[1024]{0:T(1024)S(1)} %pad_clamp_fusion), kind=kCustom, calls=%fused_computation.5 | custom fusion | bytes 4194432 | tf_op jit(solution)/shard_map/gather | solution.py:57
  46.8 3.3 %convert_bitcast_fusion.1 = bf16[16,2,2,128,128,1]{3,4,2,1,0,5:T(8,128)(2,1)} fusion(bf16[16,2,2,128,128]{4,3,2,1,0:T(8,128)(2,1)S(1)} %bitcast.101, bf16[16,2,128,128]{3,2,1,0:T(8,128)(2,1)} %param.13), kind=kOutput, calls=%fused_computation.23 | convolution fusion | flops 269484032 | bytes 5242880 | tf_op jit(solution)/shard_map/rkab,rkqbc->rkqac/dot_general | solution.py:8
  50.1 4.7 %copy.71 = bf16[16,2,2,128,128,1]{4,2,1,3,5,0:T(2,128)(2,1)S(1)} copy(bf16[16,2,2,128,128,1]{3,4,2,1,0,5:T(8,128)(2,1)} %convert_bitcast_fusion.1) | data formatting | bytes 4194304 | tf_op jit(solution)/shard_map/convert_element_type | solution.py:10
  54.8 0.1 copy.52
  54.9 0.6 gather_fusion.4
  55.5 5.8 %fusion.15 = f32[16,2,8,128,128,1]{4,2,5,3,1,0:T(8,128)S(1)} fusion(bf16[16,4,2,128,128,1]{4,1,2,3,5,0:T(4,128)(2,1)} %copy.66, s32[16,2,8]{2,1,0:T(2,128)S(1)} %copy.48, s32[16,4,2]{1,2,0:T(2,128)S(1)} %copy.47), kind=kOutput, calls=%fused_computation.27 | convolution fusion | flops 67110912 | bytes 20973056 | tf_op jit(solution)/shard_map/rpskq,rkqac->rpsac/dot_general | solution.py:13
  61.3 6.8 %fusion.11 = bf16[16,2,8,128,128]{4,2,3,1,0:T(8,128)(2,1)} fusion(f32[16,2,8,128,128,1]{4,2,5,3,1,0:T(8,128)S(1)} %fusion.15, bf16[16,2,2,128,128,1]{4,2,1,3,5,0:T(2,128)(2,1)S(1)} %copy.71, pred[16,2]{1,0:T(8,128)(4,1)S(1)} %iota_compare_fusion.2, s32[16,2,8]{2,1,0:T(2,128)S(1)} %copy.48, s32[16,2,2]{2,1,0:T(2,128)S(1)} %bitcast.104), kind=kOutput, calls=%fused_computation.18 | convolution fusion | flops 41945088 | bytes 27264288 | tf_op jit(solution)/shard_map/rpskq,rkqac->rpsac/dot_general | solution.py:13
  68.0 72.1 %while.11 = (s32[]{:T(128)}, f32[4,8,128,128]{3,0,2,1:T(4,128)}, f32[2,8,4,2]{1,2,3,0:T(4,128)S(1)}, bf16[2,8,2,8,128,128]{5,3,4,2,1,0:T(8,128)(2,1)}, bf16[2,8,...) while((s32[]{:T(128)}, f32[4,8,128,128]{3,0,2,1:T(4,128)}, ...), condition=%wide.region_1.2_spmd.clone, body=%wide.region_0.1_spmd.clone.sunk | while | flops 638582784 | bytes 59248736 | solution.py:79
  68.0 4.5 %constant_dynamic-slice_fusion.2 = bf16[1,8,2,8,128,128]{5,3,4,2,1,0:T(8,128)(2,1)} fusion(bf16[2,8,2,8,128,128]{5,3,4,2,1,0:T(8,128)(2,1)} %get-tuple-element.132, s32[]{:T(128)} %get-tuple-element.122), kind=kLoop, calls=%fused_computation.15.clone.1 | loop fusion | bytes 8388612 | tf_op jit(solution)/shard_map/while/body/jit(dynamic_index_in_dim)/dynamic_slice | solution.py:79
  72.6 6.8 %copy.87 = bf16[1,8,2,8,128,128]{4,5,3,2,1,0:T(8,128)(2,1)} copy(bf16[1,8,2,8,128,128]{5,3,4,2,1,0:T(8,128)(2,1)} %constant_dynamic-slice_fusion.2) | data formatting | bytes 8388608 | tf_op jit(solution)/shard_map/while/body/jit(dynamic_index_in_dim)/dynamic_slice | solution.py:79
  79.4 6.7 %fusion.44 = f32[8,2,8,128,128]{3,4,2,1,0:T(8,128)} fusion(bf16[1,8,2,8,128,128]{4,5,3,2,1,0:T(8,128)(2,1)} %copy.87, bf16[2,8,2,128,128]{4,3,2,1,0:T(8,128)(2,1)S(1)} %get-tuple-element.133, s32[]{:T(128)} %get-tuple-element.122), kind=kOutput, calls=%fused_computation.8.clone.1 | convolution fusion | flops 536870912 | bytes 13107204 | tf_op jit(solution)/shard_map/while/body/eval_jaxpr/rpba,rpsbc->rpsac/dot_general | solution.py:72
  86.1 9.2 %copy.88 = f32[8,2,8,128,128]{4,0,1,3,2:T(8,128)} copy(f32[8,2,8,128,128]{3,4,2,1,0:T(8,128)} %fusion.44) | data formatting | bytes 16777216 | tf_op jit(solution)/shard_map/while/body/eval_jaxpr/rpba,rpsbc->rpsac/transpose | solution.py:72
  95.2 8.7 %bitcast_add_fusion.3 = f32[4,8,128,128]{3,0,2,1:T(4,128)} fusion(f32[4,8,128,128]{3,0,2,1:T(4,128)} %get-tuple-element.123, f32[8,2,8,128,128]{4,0,1,3,2:T(8,128)} %copy.88, pred[]{:T(512)S(6)} %compare.5, f32[2,8,4,2]{1,2,3,0:T(4,128)S(1)} %get-tuple-element.131, s32[]{:T(128)} %get-tuple-element.122), kind=kOutput, calls=%fused_computation.9.clone.1 | convolution fusion | flops 101711872 | bytes 12587013 | tf_op jit(solution)/shard_map/while/body/eval_jaxpr/rgp,rpsac->gsac/dot_general | solution.py:75
  104.0 4.5 %constant_dynamic-slice_fusion.2 = bf16[1,8,2,8,128,128]{5,3,4,2,1,0:T(8,128)(2,1)} fusion(bf16[2,8,2,8,128,128]{5,3,4,2,1,0:T(8,128)(2,1)} %get-tuple-element.132, s32[]{:T(128)} %get-tuple-element.122), kind=kLoop, calls=%fused_computation.15.clone.1 | loop fusion | bytes 8388612 | tf_op jit(solution)/shard_map/while/body/jit(dynamic_index_in_dim)/dynamic_slice | solution.py:79
  108.5 6.8 %copy.87 = bf16[1,8,2,8,128,128]{4,5,3,2,1,0:T(8,128)(2,1)} copy(bf16[1,8,2,8,128,128]{5,3,4,2,1,0:T(8,128)(2,1)} %constant_dynamic-slice_fusion.2) | data formatting | bytes 8388608 | tf_op jit(solution)/shard_map/while/body/jit(dynamic_index_in_dim)/dynamic_slice | solution.py:79
  115.3 6.7 %fusion.44 = f32[8,2,8,128,128]{3,4,2,1,0:T(8,128)} fusion(bf16[1,8,2,8,128,128]{4,5,3,2,1,0:T(8,128)(2,1)} %copy.87, bf16[2,8,2,128,128]{4,3,2,1,0:T(8,128)(2,1)S(1)} %get-tuple-element.133, s32[]{:T(128)} %get-tuple-element.122), kind=kOutput, calls=%fused_computation.8.clone.1 | convolution fusion | flops 536870912 | bytes 13107204 | tf_op jit(solution)/shard_map/while/body/eval_jaxpr/rpba,rpsbc->rpsac/dot_general | solution.py:72
  122.0 9.2 %copy.88 = f32[8,2,8,128,128]{4,0,1,3,2:T(8,128)} copy(f32[8,2,8,128,128]{3,4,2,1,0:T(8,128)} %fusion.44) | data formatting | bytes 16777216 | tf_op jit(solution)/shard_map/while/body/eval_jaxpr/rpba,rpsbc->rpsac/transpose | solution.py:72
  131.2 9.0 %bitcast_add_fusion.3 = f32[4,8,128,128]{3,0,2,1:T(4,128)} fusion(f32[4,8,128,128]{3,0,2,1:T(4,128)} %get-tuple-element.123, f32[8,2,8,128,128]{4,0,1,3,2:T(8,128)} %copy.88, pred[]{:T(512)S(6)} %compare.5, f32[2,8,4,2]{1,2,3,0:T(4,128)S(1)} %get-tuple-element.131, s32[]{:T(128)} %get-tuple-element.122), kind=kOutput, calls=%fused_computation.9.clone.1 | convolution fusion | flops 101711872 | bytes 12587013 | tf_op jit(solution)/shard_map/while/body/eval_jaxpr/rgp,rpsac->gsac/dot_general | solution.py:75
  140.2 0.0 copy-start.1
  140.2 2.0 %copy.84 = bf16[4,8,128,128]{3,2,1,0:T(8,128)(2,1)S(1)} copy(f32[4,8,128,128]{3,0,2,1:T(4,128)} %get-tuple-element.40) | data formatting | bytes 3145728 | tf_op jit(solution)/shard_map/while | solution.py:79
  142.2 28.1 %all_to_all.15 = bf16[4,8,128,128]{3,2,1,0:T(8,128)(2,1)S(1)} all-to-all(bf16[4,8,128,128]{3,2,1,0:T(8,128)(2,1)S(1)} %copy.84), channel_id=1, replica_groups=mesh['group'=4,'member'=8] {'group'}, dimensions={0} | all-to-all | bytes 2097152 | tf_op jit(solution)/shard_map/all_to_all | solution.py:81
  170.3 0.9 convert_reduce_fusion
  171.2 0.0 copy-done.1
  (6 shorter events, 0.0 us)
Async XLA Ops:
  0.0 31.7 %copy-start = (bf16[16,4,128,128]{3,2,1,0:T(8,128)(2,1)S(1)}, bf16[16,4,128,128]{3,2,1,0:T(8,128)(2,1)}, u32[]{:S(2)}) copy-start(bf16[16,4,128,128]{3,2,1,0:T(8,128)(2,1)} %param.11) | copy-start | bytes 6291460
  0.0 28.0 %copy-start.2 = (bf16[16,2,128,128]{3,2,1,0:T(8,128)(2,1)S(1)}, bf16[16,2,128,128]{3,2,1,0:T(8,128)(2,1)}, u32[]{:S(2)}) copy-start(bf16[16,2,128,128]{3,2,1,0:T(8,128)(2,1)} %param.16) | copy-start | bytes 3145732
  2.8 10.3 %all-to-all-start.1 = ((s32[8,1,2]{2,1,0:T(1,128)}), s32[8,1,2]{2,1,0:T(1,128)S(1)}, u32[]{:S(2)}, u32[]{:S(2)}) async-start(s32[8,1,2]{2,1,0:T(1,128)} %bitcast.40), calls=%async_computation.1 | async-start | bytes 8192 | tf_op jit(solution)/shard_map/all_to_all | solution.py:42
  13.1 14.1 %all-to-all-start = ((bf16[8,1,2,128,128]{4,3,2,1,0:T(8,128)(2,1)}), bf16[8,1,2,128,128]{4,3,2,1,0:T(8,128)(2,1)}, u32[]{:S(2)}, u32[]{:S(2)}) async-start(bf16[8,1,2,128,128]{4,3,2,1,0:T(8,128)(2,1)} %bitcast.102), calls=%async_computation | async-start | bytes 1048576 | tf_op jit(solution)/shard_map/all_to_all | solution.py:41
  140.2 31.0 %copy-start.1 = (bf16[16,4,128,128]{3,2,1,0:T(8,128)(2,1)S(1)}, bf16[16,4,128,128]{3,2,1,0:T(8,128)(2,1)}, u32[]{:S(2)}) copy-start(bf16[16,4,128,128]{3,2,1,0:T(8,128)(2,1)} %param.11) | copy-start | bytes 6291460
where the time goes:
time: 173 us; the launch traced here: 171 us
  local copies, waits for them, and re-layouts  67 us (39%)
  matrix products  53.3 us (31%)
  blocking collectives  28.1 us (16%)
  starting transfers between devices  9.38 us (5%)
  waiting for transfers between devices  8.85 us (5%)
  other arithmetic  4.53 us (3%)
    all_to_all x1, blocking collectives, on_device(): lax.all_to_all(rounded, 'group', split_axis=0, concat_axis=0, tiled=True)  28.1 us
    dynamic_slice x4, local copies, waits for them, and re-layouts, on_device(): lax.scan(accumulate, start, (p_blocks, y_blocks, r_blocks))  22.7 us
    transpose x2, local copies, waits for them, and re-layouts, accumulate(): jnp.einsum('rpba,rpsbc->rpsac', p_part, y_part, preferred_element_type=jn...  18.4 us
    dot_general x2, matrix products, accumulate(): jnp.einsum('rgp,rpsac->gsac', r_part, products, precision=lax.Precision.H...  17.7 us
    dot_general x2, matrix products, accumulate(): jnp.einsum('rpba,rpsbc->rpsac', p_part, y_part, preferred_element_type=jn...  13.3 us
    dot_general x2, matrix products, product_terms(): jnp.einsum('rpskq,rkqac->rpsac', match.astype(jnp.bfloat16), ap_tiles, pr...  12.6 us
    convert_element_type x2, local copies, waits for them, and re-layouts, product_terms(): ap_tiles = jnp.einsum('rkab,rkqbc->rkqac', a_tiles, p_rows, preferred_ele...  12.2 us
    all_to_all x1, waiting for transfers between devices, on_device(): lax.all_to_all(out_tiles, 'member', split_axis=0, concat_axis=0, tiled=True)  8.84 us
  transfers between devices with their start and end apart: 2, of which 1 were waited for; matrix products, arithmetic and copies ran while one was open for 4% of the time, Pallas kernels for 0%

commit v1 on v0

v1 whole, which is shorter than its diff:
```python
import functools

import jax
import jax.numpy as jnp
from jax import lax
from jax.experimental import pallas as pl
from jax.experimental.pallas import tpu as pltpu
from jax.sharding import PartitionSpec as P

MESH = pl.DeviceIdType.MESH
CHUNKS = 4


def kernel(
    G,
    M,
    dcols,
    ocols,
    ocount,
    pcols,
    srows,
    ccols,
    p_hbm,
    d_hbm,
    o_hbm,
    out,
    p_v,
    d_v,
    o_v,
    pm,
    pmt,
    x,
    ar,
    sbuf,
    rbuf,
    tl,
    tt,
    gs,
    gr,
    p_sem,
    d_sem,
    o_sem,
    ms_sem,
    mr_sem,
    gs_sem,
    gr_sem,
):
    R, PT, T = p_v.shape[0], p_v.shape[1], p_v.shape[2]
    D, O = d_v.shape[1], o_v.shape[1]
    S = srows.shape[2]
    CT = ccols.shape[1]
    per = R // CHUNKS
    hoff = (0, 1, G // 2)
    moff = (M - 1, 1, M // 2)
    back = (1, 0, 2)
    coff = (0, 1, G - 1, G // 2)
    B = len(hoff)
    g = lax.axis_index("group")
    m = lax.axis_index("member")
    f32, bf16 = jnp.float32, jnp.bfloat16

    p_copy = pltpu.make_async_copy(p_hbm, p_v, p_sem)
    p_copy.start()
    for c in range(CHUNKS):
        rows = pl.ds(c * per, per)
        pltpu.make_async_copy(d_hbm.at[rows], d_v.at[rows], d_sem.at[c]).start()
    o_copy = pltpu.make_async_copy(o_hbm, o_v, o_sem)
    o_copy.start()

    barrier = pltpu.get_barrier_semaphore()
    peers = [(g, lax.rem(m + d, M)) for d in moff]
    peers += [(lax.rem(g + d, G), m) for d in (1, G - 1, G // 2)]
    for peer in peers:
        pl.semaphore_signal(barrier, inc=1, device_id=peer, device_id_type=MESH)

    own = [lax.rem(g + d, G) * M + m for d in hoff]

    p_copy.wait()
    for f in range(R):
        parts = []
        for b in range(B):
            block = jnp.zeros((T, T), bf16)
            for q in range(PT):
                block = jnp.where(pcols[f, q] == own[b], p_v[f, q], block)
            parts.append(block)
        row = jnp.concatenate(parts, axis=1)
        pm[f] = row
        pmt[:, f * T : (f + 1) * T] = row.T

    for i in range(3):
        to = lax.rem(m + moff[i], M)
        for s in range(S):
            sbuf[i, s] = pm[srows[0, to, s]]

    pl.semaphore_wait(barrier, len(peers))
    m_copies = []
    for i in range(3):
        copy = pltpu.make_async_remote_copy(
            src_ref=sbuf.at[i],
            dst_ref=rbuf.at[back[i]],
            send_sem=ms_sem.at[i],
            recv_sem=mr_sem.at[back[i]],
            device_id=(g, lax.rem(m + moff[i], M)),
            device_id_type=MESH,
        )
        copy.start()
        m_copies.append(copy)

    for c in range(CHUNKS):
        rows = pl.ds(c * per, per)
        pltpu.make_async_copy(d_hbm.at[rows], d_v.at[rows], d_sem.at[c]).wait()
        for f in range(c * per, (c + 1) * per):
            left = jnp.concatenate([d_v[f, k] for k in range(D)], axis=1)
            right = jnp.concatenate([pm[dcols[f, k]] for k in range(D)], axis=0)
            x[f * T : (f + 1) * T, :] = jnp.dot(
                left, right, preferred_element_type=f32
            ).astype(bf16)
    local = jnp.dot(pmt[...], x[...], preferred_element_type=f32)
    tl[...] = local[:T]

    sent = []
    for b in range(1, B):
        rel = [(hoff[b] + d) % G for d in coff]
        slots = [(s, hoff.index(r)) for s, r in enumerate(rel) if r in hoff]
        sent.append([s for s, _ in slots])
        for at, (_, b2) in enumerate(slots):
            gs[b - 1, at] = local[b * T : (b + 1) * T, b2 * T : (b2 + 1) * T].astype(bf16)

    def group_copy(b, part, lo, n):
        where = pl.ds(lo, n)
        return pltpu.make_async_remote_copy(
            src_ref=gs.at[b - 1, where],
            dst_ref=gr.at[b - 1, where],
            send_sem=gs_sem.at[b - 1, part],
            recv_sem=gr_sem.at[b - 1, part],
            device_id=(lax.rem(g + hoff[b], G), m),
            device_id_type=MESH,
        )

    g_copies = [[None, None] for _ in range(B)]
    for b in range(B - 1, 0, -1):
        g_copies[b][0] = group_copy(b, 0, 0, len(sent[b - 1]))
        g_copies[b][0].start()

    o_copy.wait()
    ids = [lax.rem(m + moff[i], M) * S + s for i in range(3) for s in range(S)]
    zero = jnp.zeros((T, T), bf16)
    for f in range(R):
        for r, ident in enumerate(ids):
            block = None
            for k in range(O):
                live = jnp.logical_and(ocols[f, k] == ident, ocount[f] > k)
                term = jnp.where(live, o_v[f, k], zero)
                block = term if block is None else block + term
            ar[f * T : (f + 1) * T, r * T : (r + 1) * T] = block
    mid = jnp.dot(pmt[...], ar[...], preferred_element_type=f32).astype(bf16)
    tt[3 * B] = jnp.zeros(tt.shape[1:], f32)
    for i in range(3):
        m_copies[back[i]].wait_recv()
        res = None
        for s in range(S):
            r = i * S + s
            term = jnp.dot(
                mid[:, r * T : (r + 1) * T], rbuf[i, s], preferred_element_type=f32
            )
            res = term if res is None else res + term
        for b2 in range(B):
            tt[i * B + b2] = res[:, b2 * T : (b2 + 1) * T]

    cand = [
        lax.rem(g + hoff[b2], G) * M + lax.rem(m + moff[i], M)
        for i in range(3)
        for b2 in range(B)
    ]

    def spot(b, s):
        col = ccols[own[b], s]
        at = jnp.int32(3 * B)
        for n, c in enumerate(cand):
            at = jnp.where(col == c, n, at)
        return at

    base = len(coff)
    for b in range(B - 1, 0, -1):
        lo = len(sent[b - 1])
        for s in range(base, CT):
            gs[b - 1, lo + s - base] = tt[spot(b, s), b * T : (b + 1) * T, :].astype(bf16)
        g_copies[b][1] = group_copy(b, 1, lo, CT - base)
        g_copies[b][1].start()

    for b in range(1, B):
        g_copies[b][0].wait_recv()
    rel = [d % G for d in coff]
    for s in range(base):
        total = None
        if rel[s] in hoff:
            b2 = hoff.index(rel[s])
            total = tl[:, b2 * T : (b2 + 1) * T]
        for b in range(1, B):
            if s in sent[b - 1]:
                term = gr[b - 1, sent[b - 1].index(s)].astype(f32)
                total = term if total is None else total + term
        out[0, s] = jnp.zeros((T, T), f32) if total is None else total
    for b in range(1, B):
        g_copies[b][1].wait_recv()
    for s in range(base, CT):
        total = tt[spot(0, s), :T, :]
        for b in range(1, B):
            total = total + gr[b - 1, len(sent[b - 1]) + s - base].astype(f32)
        out[0, s] = total

    for copy in m_copies:
        copy.wait_send()
    for b in range(1, B):
        for part in range(2):
            g_copies[b][part].wait_send()


def on_device(
    G,
    M,
    diag_tiles,
    diag_cols,
    offd_tiles,
    offd_cols,
    offd_count,
    p_tiles,
    p_cols,
    send_rows,
    coarse_cols,
):
    R, PT, T, _ = p_tiles.shape
    D, O = diag_tiles.shape[1], offd_tiles.shape[1]
    S = send_rows.shape[2]
    CT = coarse_cols.shape[1]
    B = 3
    bf16, f32 = jnp.bfloat16, jnp.float32
    smem = pl.BlockSpec(memory_space=pltpu.SMEM)
    hbm = pl.BlockSpec(memory_space=pl.ANY)
    return pl.pallas_call(
        functools.partial(kernel, G, M),
        out_shape=jax.ShapeDtypeStruct((1, CT, T, T), f32),
        in_specs=[smem] * 6 + [hbm] * 3,
        out_specs=pl.BlockSpec(memory_space=pltpu.VMEM),
        scratch_shapes=[
            pltpu.VMEM((R, PT, T, T), bf16),
            pltpu.VMEM((R, D, T, T), bf16),
            pltpu.VMEM((R, O, T, T), bf16),
            pltpu.VMEM((R, T, B * T), bf16),
            pltpu.VMEM((B * T, R * T), bf16),
            pltpu.VMEM((R * T, B * T), bf16),
            pltpu.VMEM((R * T, 3 * S * T), bf16),
            pltpu.VMEM((3, S, T, B * T), bf16),
            pltpu.VMEM((3, S, T, B * T), bf16),
            pltpu.VMEM((T, B * T), f32),
            pltpu.VMEM((3 * B + 1, B * T, T), f32),
            pltpu.VMEM((B - 1, CT, T, T), bf16),
            pltpu.VMEM((B - 1, CT, T, T), bf16),
            pltpu.SemaphoreType.DMA,
            pltpu.SemaphoreType.DMA((CHUNKS,)),
            pltpu.SemaphoreType.DMA,
            pltpu.SemaphoreType.DMA((3,)),
            pltpu.SemaphoreType.DMA((3,)),
            pltpu.SemaphoreType.DMA((B - 1, 2)),
            pltpu.SemaphoreType.DMA((B - 1, 2)),
        ],
        compiler_params=pltpu.CompilerParams(
            collective_id=0, has_side_effects=True, vmem_limit_bytes=63 * 1024 * 1024
        ),
    )(
        diag_cols,
        offd_cols,
        offd_count,
        p_cols,
        send_rows,
        coarse_cols,
        p_tiles,
        diag_tiles,
        offd_tiles,
    )


def solution(mesh):
    return jax.shard_map(
        functools.partial(on_device, mesh.shape["group"], mesh.shape["member"]),
        mesh=mesh,
        in_specs=(
            P(("group", "member"), None, None, None),
            P(("group", "member"), None),
            P(("group", "member"), None, None, None),
            P(("group", "member"), None),
            P(("group", "member")),
            P(("group", "member"), None, None, None),
            P(("group", "member"), None),
            P(("group", "member"), None, None),
            P(),
        ),
        out_specs=P(("group", "member"), None, None, None),
        check_vma=False,
    )
```

time: 173 us -> 36.1 us (0.21)
  local copies, waits for them, and re-layouts: 67 us -> 8.6 us
  matrix products: 53.3 us -> 0 us
  blocking collectives: 28.1 us -> 0 us
  Pallas kernels: 0 us -> 27.2 us
  starting transfers between devices: 9.38 us -> 0 us
  waiting for transfers between devices: 8.85 us -> 0 us
  other arithmetic: 4.53 us -> 0 us
    dot_general x9 -> x0, matrix products: 53.3 us -> none  [the longest x2 17.7 us: accumulate(): jnp.einsum('rgp,rpsac->gsac', r_part, products, precision=lax.Precision.H...]
    all_to_all x1 -> x0, blocking collectives: 28.1 us -> none  [on_device(): lax.all_to_all(rounded, 'group', split_axis=0, concat_axis=0, tiled=True)]
    pallas_call x0 -> x1, Pallas kernels: none -> 27.2 us  [on_device(): pl.pallas_call(functools.partial(kernel, G, M), out_shape=jax.ShapeDtypeS...]
    dynamic_slice x4 -> x0, local copies, waits for them, and re-layouts: 22.7 us -> none  [on_device(): lax.scan(accumulate, start, (p_blocks, y_blocks, r_blocks))]
    transpose x2 -> x0, local copies, waits for them, and re-layouts: 18.4 us -> none  [accumulate(): jnp.einsum('rpba,rpsbc->rpsac', p_part, y_part, preferred_element_type=jn...]
    convert_element_type x3 -> x0, local copies, waits for them, and re-layouts: 12.2 us -> none  [the longest x2 12.2 us: product_terms(): ap_tiles = jnp.einsum('rkab,rkqbc->rkqac', a_tiles, p_rows, preferred_ele...]
    gather x7 -> x0, local copies, waits for them, and re-layouts: 10.1 us -> none  [the longest x1 3.02 us: on_device(): p_tiles[diag_cols]]
    all_to_all x2 -> x0, starting transfers between devices: 9.38 us -> none  [the longest x1 5.17 us: on_device(): lax.all_to_all(out_cols, 'member', split_axis=0, concat_axis=0, tiled=True)]
  transfers between devices with their start and end apart: 2 -> 0, of which waited for: 1 -> 0; matrix products, arithmetic and copies ran while one was open for 4% -> 0% of each run, Pallas kernels for 0% -> 0%
where the time goes in v1:
time: 36.1 us; the launch traced here: 35.8 us
  Pallas kernels  27.2 us (75%)
  local copies, waits for them, and re-layouts  8.6 us (24%)
    pallas_call x1, Pallas kernels, on_device(): pl.pallas_call(functools.partial(kernel, G, M), out_shape=jax.ShapeDtypeS...  27.2 us
    unnamed x6, local copies, waits for them, and re-layouts  8.6 us

profile of v1, /device:TPU:0, one launch (start us, length us, event | category | flops | bytes accessed | tf_op | source)
XLA Modules:
  0.0 35.8 jit_solution(18040836982280184961)
XLA Ops:
  0.0 1.3 %copy.13.srows = s32[1,8,1]{2,1,0:T(8,128)} copy(s32[1,8,1]{1,2,0:T(1,128)} %param.16) | data formatting | bytes 64 | tf_op args[7]
  1.3 1.3 %copy.10.dcols = s32[16,4]{1,0:T(8,128)} copy(s32[16,4]{0,1:T(4,128)} %param.10) | data formatting | bytes 512 | tf_op args[1]
  2.7 1.3 %copy.11.ocols = s32[16,2]{1,0:T(8,128)} copy(s32[16,2]{0,1:T(2,128)} %param.12) | data formatting | bytes 256 | tf_op args[3]
  4.0 1.3 %copy.12.pcols = s32[16,2]{1,0:T(8,128)} copy(s32[16,2]{0,1:T(2,128)} %param.15) | data formatting | bytes 256 | tf_op args[6]
  5.4 1.4 %copy.14.ccols = s32[32,8]{1,0:T(8,128)} copy(s32[32,8]{0,1:T(8,128)} %param.17) | data formatting | bytes 2048 | tf_op args[8]
  6.7 27.2 %shard_map.91 = f32[1,8,128,128]{3,2,1,0:T(8,128)} custom-call(s32[16,4]{1,0:T(8,128)} %copy.10.dcols, s32[16,2]{1,0:T(8,128)} %copy.11.ocols, s32[16]{0:T(128)} %ocount.1, s32[16,2]{1,0:T(8,128)} %copy.12.pcols, s32[1,8,1]{2,1,0:T(8,128)} %copy.13.srows, s32[32,8]{1,0:T(8,128)} %copy.14.ccols, bf16[16,2,128,128]{3,2,1,0:T(8,128)(2,1)} %p_hbm.1, ...), custom_call_target="tpu_custom_call" | custom-call | tf_op jit(solution)/shard_map/pallas_call | solution.py:240
  33.9 1.9 %copy.16 = f32[1,8,128,128]{3,2,1,0:T(8,128)} copy(f32[1,8,128,128]{3,2,1,0:T(8,128)} %shard_map.91) | data formatting | bytes 1048576

commit v2 on v1

v2 whole, which is shorter than its diff:
```python
import functools

import jax
import jax.numpy as jnp
from jax import lax
from jax.experimental import pallas as pl
from jax.experimental.pallas import tpu as pltpu
from jax.sharding import PartitionSpec as P

MESH = pl.DeviceIdType.MESH
CHUNKS = 4


def kernel(
    G,
    M,
    dcols,
    ocols,
    ocount,
    pcols,
    srows,
    ccols,
    p_hbm,
    d_hbm,
    o_hbm,
    kept,
    got,
    p_v,
    d_v,
    o_v,
    pm,
    pmt,
    x,
    ar,
    sbuf,
    rbuf,
    zeros,
    kept_v,
    tt,
    gs,
    p_sem,
    d_sem,
    o_sem,
    ms_sem,
    mr_sem,
    gs_sem,
    gr_sem,
    z_sem,
    k_sem,
):
    R, PT, T = p_v.shape[0], p_v.shape[1], p_v.shape[2]
    D, O = d_v.shape[1], o_v.shape[1]
    S = srows.shape[1]
    CT = ccols.shape[0]
    per = R // CHUNKS
    hoff = (0, 1, G // 2)
    moff = (M - 1, 1, M // 2)
    back = (1, 0, 2)
    coff = (0, 1, G - 1, G // 2)
    B = len(hoff)
    g = lax.axis_index("group")
    m = lax.axis_index("member")
    f32, bf16 = jnp.float32, jnp.bfloat16

    o_copy = pltpu.make_async_copy(o_hbm, o_v, o_sem)
    p_copy = pltpu.make_async_copy(p_hbm, p_v, p_sem)
    p_copy.start()
    for c in range(CHUNKS):
        rows = pl.ds(c * per, per)
        pltpu.make_async_copy(d_hbm.at[rows], d_v.at[rows], d_sem.at[c]).start()
    o_copy.start()

    barrier = pltpu.get_barrier_semaphore()
    peers = [(g, lax.rem(m + d, M)) for d in moff]
    peers += [(lax.rem(g + d, G), m) for d in (1, G - 1, G // 2)]
    for peer in peers:
        pl.semaphore_signal(barrier, inc=1, device_id=peer, device_id_type=MESH)

    own = [lax.rem(g + d, G) * M + m for d in hoff]
    base = len(coff)

    sent = []
    for b in range(B):
        rel = [(hoff[b] + d) % G for d in coff]
        sent.append({s: hoff.index(r) for s, r in enumerate(rel) if r in hoff})
    zeros[...] = jnp.zeros((T, T), bf16)
    fills = [
        pltpu.make_async_copy(zeros, got.at[b - 1, s], z_sem.at[b - 1, s])
        for b in range(1, B)
        for s in range(base)
        if s not in sent[b]
    ]
    for fill in fills:
        fill.start()

    p_copy.wait()
    for f in range(R):
        parts = []
        for b in range(B):
            block = jnp.zeros((T, T), bf16)
            for q in range(PT):
                block = jnp.where(pcols[q, f] == own[b], p_v[f, q], block)
            parts.append(block)
        pm[f] = jnp.concatenate(parts, axis=1)

    for i in range(3):
        to = lax.rem(m + moff[i], M)
        for s in range(S):
            sbuf[i, s] = pm[srows[0, s, to]]

    pl.semaphore_wait(barrier, len(peers))
    m_copies = []
    for i in range(3):
        copy = pltpu.make_async_remote_copy(
            src_ref=sbuf.at[i],
            dst_ref=rbuf.at[back[i]],
            send_sem=ms_sem.at[i],
            recv_sem=mr_sem.at[back[i]],
            device_id=(g, lax.rem(m + moff[i], M)),
            device_id_type=MESH,
        )
        copy.start()
        m_copies.append(copy)

    ids = [lax.rem(m + moff[i], M) * S + s for i in range(3) for s in range(S)]
    zero = jnp.zeros((T, T), bf16)
    for c in range(CHUNKS):
        rows = pl.ds(c * per, per)
        pltpu.make_async_copy(d_hbm.at[rows], d_v.at[rows], d_sem.at[c]).wait()
        if c == CHUNKS - 1:
            o_copy.wait()
        for f in range(c * per, (c + 1) * per):
            left = jnp.concatenate([d_v[f, k] for k in range(D)], axis=1)
            right = jnp.concatenate([pm[dcols[k, f]] for k in range(D)], axis=0)
            x[f * T : (f + 1) * T, :] = jnp.dot(
                left, right, preferred_element_type=f32
            ).astype(bf16)
            pmt[:, f * T : (f + 1) * T] = pm[f].T
    local = jnp.dot(pmt[T:, :], x[...], preferred_element_type=f32)

    def group_copy(b, lo, n):
        where = pl.ds(lo, n)
        return pltpu.make_async_remote_copy(
            src_ref=gs.at[b - 1, where],
            dst_ref=got.at[b - 1, where],
            send_sem=gs_sem.at[b - 1, lo],
            recv_sem=gr_sem.at[b - 1, lo],
            device_id=(lax.rem(g + hoff[b], G), m),
            device_id_type=MESH,
        )

    g_copies = []
    for b in range(B - 1, 0, -1):
        for s, b2 in sent[b].items():
            gs[b - 1, s] = local[(b - 1) * T : b * T, b2 * T : (b2 + 1) * T].astype(bf16)
        lo = 0
        while lo < base:
            n = 0
            while lo + n < base and lo + n in sent[b]:
                n += 1
            if n:
                g_copies.append(group_copy(b, lo, n))
                g_copies[-1].start()
            lo += n + 1

    for f in range(R):
        for r, ident in enumerate(ids):
            block = None
            for k in range(O):
                live = jnp.logical_and(ocols[k, f] == ident, ocount[f] > k)
                term = jnp.where(live, o_v[f, k], zero)
                block = term if block is None else block + term
            ar[f * T : (f + 1) * T, r * T : (r + 1) * T] = block
    tt[3 * B] = jnp.zeros(tt.shape[1:], f32)

    def remote(lo, hi, arrive):
        mid = jnp.dot(pmt[lo:hi, :], ar[...], preferred_element_type=f32).astype(bf16)
        for i in range(3):
            if arrive:
                m_copies[back[i]].wait_recv()
            res = None
            for s in range(S):
                r = i * S + s
                term = jnp.dot(
                    mid[:, r * T : (r + 1) * T], rbuf[i, s], preferred_element_type=f32
                )
                res = term if res is None else res + term
            for b2 in range(B):
                tt[i * B + b2, lo:hi] = res[:, b2 * T : (b2 + 1) * T]

    cand = [
        lax.rem(g + hoff[b2], G) * M + lax.rem(m + moff[i], M)
        for i in range(3)
        for b2 in range(B)
    ]

    def spot(b, s):
        col = ccols[s, own[b]]
        at = jnp.int32(3 * B)
        for n, c in enumerate(cand):
            at = jnp.where(col == c, n, at)
        return at

    remote(T, B * T, True)
    for b in range(B - 1, 0, -1):
        for s in range(base, CT):
            gs[b - 1, s] = tt[spot(b, s), b * T : (b + 1) * T, :].astype(bf16)
        g_copies.append(group_copy(b, base, CT - base))
        g_copies[-1].start()

    local = jnp.dot(pmt[:T, :], x[...], preferred_element_type=f32)
    for s in range(base):
        if s in sent[0]:
            b2 = sent[0][s]
            kept_v[s] = local[:, b2 * T : (b2 + 1) * T]
        else:
            kept_v[s] = jnp.zeros((T, T), f32)
    remote(0, T, False)
    for s in range(base, CT):
        kept_v[s] = tt[spot(0, s), :T, :]
    keep = pltpu.make_async_copy(kept_v, kept, k_sem)
    keep.start()

    for fill in fills:
        fill.wait()
    keep.wait()
    for copy in m_copies:
        copy.wait_send()
    for copy in g_copies:
        copy.wait()


def on_device(
    G,
    M,
    diag_tiles,
    diag_cols,
    offd_tiles,
    offd_cols,
    offd_count,
    p_tiles,
    p_cols,
    send_rows,
    coarse_cols,
):
    R, PT, T, _ = p_tiles.shape
    D, O = diag_tiles.shape[1], offd_tiles.shape[1]
    S = send_rows.shape[2]
    CT = coarse_cols.shape[1]
    B = 3
    bf16, f32 = jnp.bfloat16, jnp.float32
    smem = pl.BlockSpec(memory_space=pltpu.SMEM)
    hbm = pl.BlockSpec(memory_space=pl.ANY)
    kept, got = pl.pallas_call(
        functools.partial(kernel, G, M),
        out_shape=(
            jax.ShapeDtypeStruct((CT, T, T), f32),
            jax.ShapeDtypeStruct((B - 1, CT, T, T), bf16),
        ),
        in_specs=[smem] * 6 + [hbm] * 3,
        out_specs=(hbm, hbm),
        scratch_shapes=[
            pltpu.VMEM((R, PT, T, T), bf16),
            pltpu.VMEM((R, D, T, T), bf16),
            pltpu.VMEM((R, O, T, T), bf16),
            pltpu.VMEM((R, T, B * T), bf16),
            pltpu.VMEM((B * T, R * T), bf16),
            pltpu.VMEM((R * T, B * T), bf16),
            pltpu.VMEM((R * T, 3 * S * T), bf16),
            pltpu.VMEM((3, S, T, B * T), bf16),
            pltpu.VMEM((3, S, T, B * T), bf16),
            pltpu.VMEM((T, T), bf16),
            pltpu.VMEM((CT, T, T), f32),
            pltpu.VMEM((3 * B + 1, B * T, T), f32),
            pltpu.VMEM((B - 1, CT, T, T), bf16),
            pltpu.SemaphoreType.DMA,
            pltpu.SemaphoreType.DMA((CHUNKS,)),
            pltpu.SemaphoreType.DMA,
            pltpu.SemaphoreType.DMA((3,)),
            pltpu.SemaphoreType.DMA((3,)),
            pltpu.SemaphoreType.DMA((B - 1, CT)),
            pltpu.SemaphoreType.DMA((B - 1, CT)),
            pltpu.SemaphoreType.DMA((B - 1, CT)),
            pltpu.SemaphoreType.DMA,
        ],
        compiler_params=pltpu.CompilerParams(
            collective_id=0, has_side_effects=True, vmem_limit_bytes=63 * 1024 * 1024
        ),
    )(
        diag_cols.T,
        offd_cols.T,
        offd_count,
        p_cols.T,
        jnp.swapaxes(send_rows, 1, 2),
        coarse_cols.T,
        p_tiles,
        diag_tiles,
        offd_tiles,
    )
    return (kept + got[0].astype(f32) + got[1].astype(f32))[None]


def solution(mesh):
    return jax.shard_map(
        functools.partial(on_device, mesh.shape["group"], mesh.shape["member"]),
        mesh=mesh,
        in_specs=(
            P(("group", "member"), None, None, None),
            P(("group", "member"), None),
            P(("group", "member"), None, None, None),
            P(("group", "member"), None),
            P(("group", "member")),
            P(("group", "member"), None, None, None),
            P(("group", "member"), None),
            P(("group", "member"), None, None),
            P(),
        ),
        out_specs=P(("group", "member"), None, None, None),
        check_vma=False,
    )
```

time: 36.1 us -> 27.6 us (0.76)
  local copies, waits for them, and re-layouts: 8.6 us -> 0 us
  other arithmetic: 0 us -> 2.06 us
  Pallas kernels: 27.2 us -> 25.4 us
    unnamed x6 -> x0, local copies, waits for them, and re-layouts: 8.6 us -> none
    broadcast_in_dim x0 -> x1, other arithmetic: none -> 2.06 us  [on_device(): return (kept + got[0].astype(f32) + got[1].astype(f32))[None]]
    pallas_call x1, Pallas kernels: 27.2 us -> 25.4 us  [on_device(): pl.pallas_call(functools.partial(kernel, G, M), out_shape=(jax.ShapeDtype...]
where the time goes in v2:
time: 27.6 us; the launch traced here: 27.4 us
  Pallas kernels  25.4 us (92%)
  other arithmetic  2.06 us (7%)
    pallas_call x1, Pallas kernels, on_device(): pl.pallas_call(functools.partial(kernel, G, M), out_shape=(jax.ShapeDtype...  25.4 us
    broadcast_in_dim x1, other arithmetic, on_device(): return (kept + got[0].astype(f32) + got[1].astype(f32))[None]  2.06 us

profile of v2, /device:TPU:0, one launch (start us, length us, event | category | flops | bytes accessed | tf_op | source)
XLA Modules:
  0.0 27.4 jit_solution(1191667541672641044)
XLA Ops:
  0.0 25.4 %shard_map.91 = (f32[8,128,128]{2,1,0:T(8,128)}, bf16[2,8,128,128]{3,2,1,0:T(8,128)(2,1)}) custom-call(s32[4,16]{1,0:T(4,128)} %bitcast.14, s32[2,16]{1,0:T(2,128)} %bitcast.15, s32[16]{0:T(128)} %ocount.1, s32[2,16]{1,0:T(2,128)} %bitcast.16, s32[1,1,8]{2,1,0:T(1,128)} %bitcast.17, s32[8,32]{1,0:T(8,128)} %bitcast.13, bf16[16,2,128,128]{3,2,1,0:T(8,128)(2,1)} %p_hbm.1, ...), custom_call_target="tpu_custom_call" | custom-call | tf_op jit(solution)/shard_map/pallas_call | solution.py:254
  25.4 2.1 %fusion = f32[1,8,128,128]{3,2,1,0:T(8,128)} fusion(f32[8,128,128]{2,1,0:T(8,128)} %get-tuple-element.7, bf16[2,8,128,128]{3,2,1,0:T(8,128)(2,1)} %get-tuple-element.8), kind=kLoop, calls=%fused_computation.1 | loop fusion | flops 524288 | bytes 1572864 | tf_op jit(solution)/shard_map/broadcast_in_dim | solution.py:300

commit v3 on v2

--- a/solution.py
+++ b/solution.py
@@ -38,6 +38,8 @@
     kept_v,
     tt,
     gs,
+    loc,
+    fed_v,
     p_sem,
     d_sem,
     o_sem,
@@ -47,6 +49,7 @@
     gr_sem,
     z_sem,
     k_sem,
+    f_sem,
 ):
     R, PT, T = p_v.shape[0], p_v.shape[1], p_v.shape[2]
     D, O = d_v.shape[1], o_v.shape[1]
@@ -83,15 +86,43 @@
     for b in range(B):
         rel = [(hoff[b] + d) % G for d in coff]
         sent.append({s: hoff.index(r) for s, r in enumerate(rel) if r in hoff})
-    zeros[...] = jnp.zeros((T, T), bf16)
-    fills = [
-        pltpu.make_async_copy(zeros, got.at[b - 1, s], z_sem.at[b - 1, s])
-        for b in range(1, B)
-        for s in range(base)
-        if s not in sent[b]
-    ]
-    for fill in fills:
-        fill.start()
+    relays = {1: 1, 2: 2} if G == 4 else {}
+    feeds = {1: 3, 2: 0} if G == 4 else {}
+
+    def runs(have):
+        found = []
+        for s in sorted(have):
+            if found and sum(found[-1]) == s:
+                found[-1] = (found[-1][0], found[-1][1] + 1)
+            else:
+                found.append((s, 1))
+        return found
+
+    def fill(b, lo, n):
+        where = pl.ds(lo, n)
+        return pltpu.make_async_copy(zeros.at[pl.ds(0, n)], got.at[b - 1, where], z_sem.at[b - 1, lo])
+
+    def each_fill(act):
+        for b in range(1, B):
+            gap = runs(set(range(base)) - set(sent[b]))
+
+            def some(b=b, gap=gap):
+                for lo, n in gap:
+                    act(fill(b, lo, n))
+
+            if not relays:
+                some()
+                continue
+            fed = (relays[b] + hoff[b]) % G
+            other = B - b
+            pl.when(jnp.logical_and(g != (relays[other] + hoff[other]) % G, g != fed))(some)
+
+            @pl.when(g == fed)
+            def _(other=other):
+                act(fill(other, 0, CT))
+
+    zeros[...] = jnp.zeros((CT, T, T), bf16)
+    each_fill(lambda copy: copy.start())
 
     p_copy.wait()
     for f in range(R):
@@ -149,19 +180,63 @@
             device_id_type=MESH,
         )
 
-    g_copies = []
+    def feed_copy(b, lo, n):
+        where = pl.ds(lo, n)
+        return pltpu.make_async_remote_copy(
+            src_ref=gs.at[b - 1, where],
+            dst_ref=fed_v.at[where],
+            send_sem=gs_sem.at[b - 1, lo],
+            recv_sem=f_sem.at[lo],
+            device_id=(relays[B - b], m),
+            device_id_type=MESH,
+        )
+
+    last = [(base, CT - base)]
+
+    def each_send(b, spans, act):
+        def direct():
+            for lo, n in spans:
+                act(group_copy(b, lo, n))
+
+        if not relays:
+            direct()
+            return
+        pl.when(jnp.logical_and(g != feeds[b], g != relays[b]))(direct)
+
+        @pl.when(g == feeds[b])
+        def _():
+            for lo, n in spans:
+                act(feed_copy(b, lo, n))
+
+    def each_relay(first, act):
+        for b in relays:
+            pl.when(g == relays[b])(functools.partial(act, b, first))
+
+    def add_and_send(b, first):
+        spans = runs(sent[B - b]) if first else last
+        for lo, n in spans:
+            feed_copy(B - b, lo, n).wait_recv()
+        lo, n = (0, base) if first else last[0]
+        come = [s for at, count in spans for s in range(at, at + count)]
+        for s in range(lo, lo + n):
+            total = None
+            if not first:
+                total = tt[spot(b, s), b * T : (b + 1) * T, :]
+            elif s in sent[b]:
+                b2 = sent[b][s]
+                total = loc[(b - 1) * T : b * T, b2 * T : (b2 + 1) * T]
+            if s in come:
+                term = fed_v[s].astype(f32)
+                total = term if total is None else total + term
+            gs[b - 1, s] = total.astype(bf16)
+        group_copy(b, lo, n).start()
+
+    if relays:
+        loc[...] = local
     for b in range(B - 1, 0, -1):
         for s, b2 in sent[b].items():
             gs[b - 1, s] = local[(b - 1) * T : b * T, b2 * T : (b2 + 1) * T].astype(bf16)
-        lo = 0
-        while lo < base:
-            n = 0
-            while lo + n < base and lo + n in sent[b]:
-                n += 1
-            if n:
-                g_copies.append(group_copy(b, lo, n))
-                g_copies[-1].start()
-            lo += n + 1
+        each_send(b, runs(sent[b]), lambda copy: copy.start())
 
     for f in range(R):
         for r, ident in enumerate(ids):
@@ -205,8 +280,8 @@
     for b in range(B - 1, 0, -1):
         for s in range(base, CT):
             gs[b - 1, s] = tt[spot(b, s), b * T : (b + 1) * T, :].astype(bf16)
-        g_copies.append(group_copy(b, base, CT - base))
-        g_copies[-1].start()
+        each_send(b, last, lambda copy: copy.start())
+    each_relay(True, add_and_send)
 
     local = jnp.dot(pmt[:T, :], x[...], preferred_element_type=f32)
     for s in range(base):
@@ -221,13 +296,36 @@
     keep = pltpu.make_async_copy(kept_v, kept, k_sem)
     keep.start()
 
-    for fill in fills:
-        fill.wait()
+    each_relay(False, add_and_send)
+
+    each_fill(lambda copy: copy.wait())
     keep.wait()
     for copy in m_copies:
         copy.wait_send()
-    for copy in g_copies:
-        copy.wait()
+    for b in range(1, B):
+        each_send(b, runs(sent[b]) + last, lambda copy: copy.wait_send())
+        if not relays:
+            for lo, n in runs(sent[b]) + last:
+                group_copy(b, lo, n).wait_recv()
+            continue
+        whole = [(0, base)] + last
+
+        @pl.when(g == relays[b])
+        def _(b=b):
+            for lo, n in whole:
+                group_copy(b, lo, n).wait_send()
+
+        fed = (relays[b] + hoff[b]) % G
+
+        @pl.when(g == fed)
+        def _(b=b):
+            for lo, n in whole:
+                group_copy(b, lo, n).wait_recv()
+
+        @pl.when(lax.rem(g, 2) == 1)
+        def _(b=b):
+            for lo, n in runs(sent[b]) + last:
+                group_copy(b, lo, n).wait_recv()
 
 
 def on_device(
@@ -269,10 +367,12 @@
             pltpu.VMEM((R * T, 3 * S * T), bf16),
             pltpu.VMEM((3, S, T, B * T), bf16),
             pltpu.VMEM((3, S, T, B * T), bf16),
-            pltpu.VMEM((T, T), bf16),
+            pltpu.VMEM((CT, T, T), bf16),
             pltpu.VMEM((CT, T, T), f32),
             pltpu.VMEM((3 * B + 1, B * T, T), f32),
             pltpu.VMEM((B - 1, CT, T, T), bf16),
+            pltpu.VMEM(((B - 1) * T, B * T), f32),
+            pltpu.VMEM((CT, T, T), bf16),
             pltpu.SemaphoreType.DMA,
             pltpu.SemaphoreType.DMA((CHUNKS,)),
             pltpu.SemaphoreType.DMA,
@@ -282,6 +382,7 @@
             pltpu.SemaphoreType.DMA((B - 1, CT)),
             pltpu.SemaphoreType.DMA((B - 1, CT)),
             pltpu.SemaphoreType.DMA,
+            pltpu.SemaphoreType.DMA((CT,)),
         ],
         compiler_params=pltpu.CompilerParams(
             collective_id=0, has_side_effects=True, vmem_limit_bytes=63 * 1024 * 1024

time: 27.6 us -> 27.3 us (0.989)
  Pallas kernels: 25.4 us -> 25.1 us
where the time goes in v3:
time: 27.3 us; the launch traced here: 27.2 us
  Pallas kernels  25.1 us (92%)
  other arithmetic  2.06 us (8%)
    pallas_call x1, Pallas kernels, on_device(): pl.pallas_call(functools.partial(kernel, G, M), out_shape=(jax.ShapeDtype...  25.1 us
    broadcast_in_dim x1, other arithmetic, on_device(): return (kept + got[0].astype(f32) + got[1].astype(f32))[None]  2.06 us

profile of v3, /device:TPU:0, one launch (start us, length us, event | category | flops | bytes accessed | tf_op | source)
XLA Modules:
  0.0 27.2 jit_solution(1184407658891032882)
XLA Ops:
  0.0 25.1 %shard_map.91 = (f32[8,128,128]{2,1,0:T(8,128)}, bf16[2,8,128,128]{3,2,1,0:T(8,128)(2,1)}) custom-call(s32[4,16]{1,0:T(4,128)} %bitcast.14, s32[2,16]{1,0:T(2,128)} %bitcast.15, s32[16]{0:T(128)} %ocount.1, s32[2,16]{1,0:T(2,128)} %bitcast.16, s32[1,1,8]{2,1,0:T(1,128)} %bitcast.17, s32[8,32]{1,0:T(8,128)} %bitcast.13, bf16[16,2,128,128]{3,2,1,0:T(8,128)(2,1)} %p_hbm.1, ...), custom_call_target="tpu_custom_call" | custom-call | tf_op jit(solution)/shard_map/pallas_call | solution.py:352
  25.1 2.1 %fusion = f32[1,8,128,128]{3,2,1,0:T(8,128)} fusion(f32[8,128,128]{2,1,0:T(8,128)} %get-tuple-element.7, bf16[2,8,128,128]{3,2,1,0:T(8,128)(2,1)} %get-tuple-element.8), kind=kLoop, calls=%fused_computation.1 | loop fusion | flops 524288 | bytes 1572864 | tf_op jit(solution)/shard_map/broadcast_in_dim | solution.py:401

commit v4 on v3

--- a/solution.py
+++ b/solution.py
@@ -153,22 +153,6 @@
         copy.start()
         m_copies.append(copy)
 
-    ids = [lax.rem(m + moff[i], M) * S + s for i in range(3) for s in range(S)]
-    zero = jnp.zeros((T, T), bf16)
-    for c in range(CHUNKS):
-        rows = pl.ds(c * per, per)
-        pltpu.make_async_copy(d_hbm.at[rows], d_v.at[rows], d_sem.at[c]).wait()
-        if c == CHUNKS - 1:
-            o_copy.wait()
-        for f in range(c * per, (c + 1) * per):
-            left = jnp.concatenate([d_v[f, k] for k in range(D)], axis=1)
-            right = jnp.concatenate([pm[dcols[k, f]] for k in range(D)], axis=0)
-            x[f * T : (f + 1) * T, :] = jnp.dot(
-                left, right, preferred_element_type=f32
-            ).astype(bf16)
-            pmt[:, f * T : (f + 1) * T] = pm[f].T
-    local = jnp.dot(pmt[T:, :], x[...], preferred_element_type=f32)
-
     def group_copy(b, lo, n):
         where = pl.ds(lo, n)
         return pltpu.make_async_remote_copy(
@@ -191,11 +175,19 @@
             device_id_type=MESH,
         )
 
-    last = [(base, CT - base)]
-
-    def each_send(b, spans, act):
+    cols = ((0, 1), (2,))
+    spans = {
+        b: [runs(s for s, b2 in sent[b].items() if b2 in part) for part in cols]
+        for b in range(1, B)
+    }
+    half = (CT - base) // 2
+    rest = [(base, half), (base + half, CT - base - half)]
+    full = {b: spans[b][0] + spans[b][1] + rest for b in range(1, B)}
+    alone = {b: runs(set(range(base)) - set(sent[B - b])) for b in relays}
+
+    def each_send(b, which, act):
         def direct():
-            for lo, n in spans:
+            for lo, n in which:
                 act(group_copy(b, lo, n))
 
         if not relays:
@@ -205,51 +197,70 @@
 
         @pl.when(g == feeds[b])
         def _():
-            for lo, n in spans:
+            for lo, n in which:
                 act(feed_copy(b, lo, n))
 
-    def each_relay(first, act):
-        for b in relays:
-            pl.when(g == relays[b])(functools.partial(act, b, first))
-
-    def add_and_send(b, first):
-        spans = runs(sent[B - b]) if first else last
-        for lo, n in spans:
+    def start(b, which):
+        each_send(b, which, lambda copy: copy.start())
+
+    def add_and_send(b, lo, n, come):
+        if come:
             feed_copy(B - b, lo, n).wait_recv()
-        lo, n = (0, base) if first else last[0]
-        come = [s for at, count in spans for s in range(at, at + count)]
         for s in range(lo, lo + n):
             total = None
-            if not first:
+            if s >= base:
                 total = tt[spot(b, s), b * T : (b + 1) * T, :]
             elif s in sent[b]:
-                b2 = sent[b][s]
-                total = loc[(b - 1) * T : b * T, b2 * T : (b2 + 1) * T]
-            if s in come:
+                total = loc[(b - 1) * T : b * T, sent[b][s] * T : (sent[b][s] + 1) * T]
+            if come:
                 term = fed_v[s].astype(f32)
                 total = term if total is None else total + term
             gs[b - 1, s] = total.astype(bf16)
         group_copy(b, lo, n).start()
 
-    if relays:
-        loc[...] = local
-    for b in range(B - 1, 0, -1):
+    def relay(part):
+        for b in relays:
+
+            @pl.when(g == relays[b])
+            def _(b=b):
+                for lo, n in rest if part == 2 else spans[B - b][part]:
+                    add_and_send(b, lo, n, True)
+                if part == 1:
+                    for lo, n in alone[b]:
+                        add_and_send(b, lo, n, False)
+
+    def local_part(part):
+        at = slice(cols[part][0] * T, (cols[part][-1] + 1) * T)
+        for c in range(CHUNKS):
+            if part == 0:
+                rows = pl.ds(c * per, per)
+                pltpu.make_async_copy(d_hbm.at[rows], d_v.at[rows], d_sem.at[c]).wait()
+            for f in range(c * per, (c + 1) * per):
+                left = jnp.concatenate([d_v[f, k] for k in range(D)], axis=1)
+                right = jnp.concatenate([pm[dcols[k, f], :, at] for k in range(D)], axis=0)
+                x[f * T : (f + 1) * T, at] = jnp.dot(
+                    left, right, preferred_element_type=f32
+                ).astype(bf16)
+                if part == 0:
+                    pmt[:, f * T : (f + 1) * T] = pm[f].T
+        loc[:, at] = jnp.dot(pmt[T:, :], x[:, at], preferred_element_type=f32)
+
+    def stage(b, part):
         for s, b2 in sent[b].items():
-            gs[b - 1, s] = local[(b - 1) * T : b * T, b2 * T : (b2 + 1) * T].astype(bf16)
-        each_send(b, runs(sent[b]), lambda copy: copy.start())
-
-    for f in range(R):
-        for r, ident in enumerate(ids):
-            block = None
-            for k in range(O):
-                live = jnp.logical_and(ocols[k, f] == ident, ocount[f] > k)
-                term = jnp.where(live, o_v[f, k], zero)
-                block = term if block is None else block + term
-            ar[f * T : (f + 1) * T, r * T : (r + 1) * T] = block
-    tt[3 * B] = jnp.zeros(tt.shape[1:], f32)
-
-    def remote(lo, hi, arrive):
-        mid = jnp.dot(pmt[lo:hi, :], ar[...], preferred_element_type=f32).astype(bf16)
+            if b2 in cols[part]:
+                gs[b - 1, s] = loc[(b - 1) * T : b * T, b2 * T : (b2 + 1) * T].astype(bf16)
+
+    def stage_rest(b):
+        for s in range(base, CT):
+            gs[b - 1, s] = tt[spot(b, s), b * T : (b + 1) * T, :].astype(bf16)
+
+    ids = [lax.rem(m + moff[i], M) * S + s for i in range(3) for s in range(S)]
+    zero = jnp.zeros((T, T), bf16)
+
+    def remote_mid(lo, hi):
+        return jnp.dot(pmt[lo:hi, :], ar[...], preferred_element_type=f32).astype(bf16)
+
+    def remote(mid, lo, hi, arrive):
         for i in range(3):
             if arrive:
                 m_copies[back[i]].wait_recv()
@@ -276,12 +287,35 @@
             at = jnp.where(col == c, n, at)
         return at
 
-    remote(T, B * T, True)
-    for b in range(B - 1, 0, -1):
-        for s in range(base, CT):
-            gs[b - 1, s] = tt[spot(b, s), b * T : (b + 1) * T, :].astype(bf16)
-        each_send(b, last, lambda copy: copy.start())
-    each_relay(True, add_and_send)
+    local_part(0)
+    stage(1, 0)
+    start(1, spans[1][0])
+
+    o_copy.wait()
+    for f in range(R):
+        for r, ident in enumerate(ids):
+            block = None
+            for k in range(O):
+                live = jnp.logical_and(ocols[k, f] == ident, ocount[f] > k)
+                term = jnp.where(live, o_v[f, k], zero)
+                block = term if block is None else block + term
+            ar[f * T : (f + 1) * T, r * T : (r + 1) * T] = block
+    mid = remote_mid(T, B * T)
+    stage(2, 0)
+    start(2, spans[2][0])
+
+    tt[3 * B] = jnp.zeros(tt.shape[1:], f32)
+    remote(mid, T, B * T, True)
+    stage_rest(1)
+    start(1, rest)
+    local_part(1)
+    stage(1, 1)
+    start(1, spans[1][1])
+    stage_rest(2)
+    start(2, rest)
+    stage(2, 1)
+    start(2, spans[2][1])
+    relay(0)
 
     local = jnp.dot(pmt[:T, :], x[...], preferred_element_type=f32)
     for s in range(base):
@@ -290,41 +324,39 @@
             kept_v[s] = local[:, b2 * T : (b2 + 1) * T]
         else:
             kept_v[s] = jnp.zeros((T, T), f32)
-    remote(0, T, False)
+    remote(remote_mid(0, T), 0, T, False)
     for s in range(base, CT):
         kept_v[s] = tt[spot(0, s), :T, :]
     keep = pltpu.make_async_copy(kept_v, kept, k_sem)
     keep.start()
-
-    each_relay(False, add_and_send)
+    relay(2)
+    relay(1)
 
     each_fill(lambda copy: copy.wait())
     keep.wait()
     for copy in m_copies:
         copy.wait_send()
     for b in range(1, B):
-        each_send(b, runs(sent[b]) + last, lambda copy: copy.wait_send())
+        each_send(b, full[b], lambda copy: copy.wait_send())
         if not relays:
-            for lo, n in runs(sent[b]) + last:
+            for lo, n in full[b]:
                 group_copy(b, lo, n).wait_recv()
             continue
-        whole = [(0, base)] + last
+        whole = spans[B - b][0] + spans[B - b][1] + alone[b] + rest
 
         @pl.when(g == relays[b])
-        def _(b=b):
+        def _(b=b, whole=whole):
             for lo, n in whole:
                 group_copy(b, lo, n).wait_send()
 
-        fed = (relays[b] + hoff[b]) % G
-
-        @pl.when(g == fed)
-        def _(b=b):
+        @pl.when(g == (relays[b] + hoff[b]) % G)
+        def _(b=b, whole=whole):
             for lo, n in whole:
                 group_copy(b, lo, n).wait_recv()
 
         @pl.when(lax.rem(g, 2) == 1)
         def _(b=b):
-            for lo, n in runs(sent[b]) + last:
+            for lo, n in full[b]:
                 group_copy(b, lo, n).wait_recv()
 
 

time: 27.3 us -> 26.6 us (0.974)
  Pallas kernels: 25.1 us -> 24.3 us
    pallas_call x1, Pallas kernels: 25.1 us -> 24.3 us  [on_device(): pl.pallas_call(functools.partial(kernel, G, M), out_shape=(jax.ShapeDtype...]
where the time goes in v4:
time: 26.6 us; the launch traced here: 26.4 us
  Pallas kernels  24.3 us (91%)
  other arithmetic  2.06 us (8%)
    pallas_call x1, Pallas kernels, on_device(): pl.pallas_call(functools.partial(kernel, G, M), out_shape=(jax.ShapeDtype...  24.3 us
    broadcast_in_dim x1, other arithmetic, on_device(): return (kept + got[0].astype(f32) + got[1].astype(f32))[None]  2.06 us

profile of v4, /device:TPU:0, one launch (start us, length us, event | category | flops | bytes accessed | tf_op | source)
XLA Modules:
  0.0 26.4 jit_solution(2162454941193399912)
XLA Ops:
  0.0 24.3 %shard_map.91 = (f32[8,128,128]{2,1,0:T(8,128)}, bf16[2,8,128,128]{3,2,1,0:T(8,128)(2,1)}) custom-call(s32[4,16]{1,0:T(4,128)} %bitcast.14, s32[2,16]{1,0:T(2,128)} %bitcast.15, s32[16]{0:T(128)} %ocount.1, s32[2,16]{1,0:T(2,128)} %bitcast.16, s32[1,1,8]{2,1,0:T(1,128)} %bitcast.17, s32[8,32]{1,0:T(8,128)} %bitcast.13, bf16[16,2,128,128]{3,2,1,0:T(8,128)(2,1)} %p_hbm.1, ...), custom_call_target="tpu_custom_call" | custom-call | tf_op jit(solution)/shard_map/pallas_call | solution.py:384
  24.3 2.1 %fusion = f32[1,8,128,128]{3,2,1,0:T(8,128)} fusion(f32[8,128,128]{2,1,0:T(8,128)} %get-tuple-element.7, bf16[2,8,128,128]{3,2,1,0:T(8,128)(2,1)} %get-tuple-element.8), kind=kLoop, calls=%fused_computation.1 | loop fusion | flops 524288 | bytes 1572864 | tf_op jit(solution)/shard_map/broadcast_in_dim | solution.py:433

commit v5 on v4

--- a/solution.py
+++ b/solution.py
@@ -14,12 +14,12 @@
 def kernel(
     G,
     M,
-    dcols,
-    ocols,
-    ocount,
-    pcols,
-    srows,
-    ccols,
+    dcols_hbm,
+    ocols_hbm,
+    ocount_hbm,
+    pcols_hbm,
+    srows_hbm,
+    ccols_hbm,
     p_hbm,
     d_hbm,
     o_hbm,
@@ -40,6 +40,13 @@
     gs,
     loc,
     fed_v,
+    dcols,
+    ocols,
+    ocount,
+    pcols,
+    srows,
+    ccols,
+    i_sem,
     p_sem,
     d_sem,
     o_sem,
@@ -65,9 +72,17 @@
     m = lax.axis_index("member")
     f32, bf16 = jnp.float32, jnp.bfloat16
 
+    ints = ((pcols_hbm, pcols), (srows_hbm, srows), (dcols_hbm, dcols))
+    ints += ((ocols_hbm, ocols), (ocount_hbm, ocount), (ccols_hbm, ccols))
+    i_copies = [pltpu.make_async_copy(a, b, i_sem.at[n]) for n, (a, b) in enumerate(ints)]
+    for copy in i_copies:
+        copy.start()
     o_copy = pltpu.make_async_copy(o_hbm, o_v, o_sem)
-    p_copy = pltpu.make_async_copy(p_hbm, p_v, p_sem)
-    p_copy.start()
+    p_copies = []
+    for c in range(CHUNKS):
+        rows = pl.ds(c * per, per)
+        p_copies.append(pltpu.make_async_copy(p_hbm.at[rows], p_v.at[rows], p_sem.at[c]))
+        p_copies[-1].start()
     for c in range(CHUNKS):
         rows = pl.ds(c * per, per)
         pltpu.make_async_copy(d_hbm.at[rows], d_v.at[rows], d_sem.at[c]).start()
@@ -124,8 +139,11 @@
     zeros[...] = jnp.zeros((CT, T, T), bf16)
     each_fill(lambda copy: copy.start())
 
-    p_copy.wait()
+    for copy in i_copies:
+        copy.wait()
     for f in range(R):
+        if f % per == 0:
+            p_copies[f // per].wait()
         parts = []
         for b in range(B):
             block = jnp.zeros((T, T), bf16)
@@ -139,10 +157,8 @@
         for s in range(S):
             sbuf[i, s] = pm[srows[0, s, to]]
 
-    pl.semaphore_wait(barrier, len(peers))
-    m_copies = []
-    for i in range(3):
-        copy = pltpu.make_async_remote_copy(
+    m_copies = [
+        pltpu.make_async_remote_copy(
             src_ref=sbuf.at[i],
             dst_ref=rbuf.at[back[i]],
             send_sem=ms_sem.at[i],
@@ -150,8 +166,13 @@
             device_id=(g, lax.rem(m + moff[i], M)),
             device_id_type=MESH,
         )
-        copy.start()
-        m_copies.append(copy)
+        for i in range(3)
+    ]
+
+    def enter():
+        pl.semaphore_wait(barrier, len(peers))
+        for copy in m_copies:
+            copy.start()
 
     def group_copy(b, lo, n):
         where = pl.ds(lo, n)
@@ -243,6 +264,8 @@
                 ).astype(bf16)
                 if part == 0:
                     pmt[:, f * T : (f + 1) * T] = pm[f].T
+            if part == 0 and c == CHUNKS - 2:
+                enter()
         loc[:, at] = jnp.dot(pmt[T:, :], x[:, at], preferred_element_type=f32)
 
     def stage(b, part):
@@ -324,13 +347,13 @@
             kept_v[s] = local[:, b2 * T : (b2 + 1) * T]
         else:
             kept_v[s] = jnp.zeros((T, T), f32)
+    relay(2)
+    relay(1)
     remote(remote_mid(0, T), 0, T, False)
     for s in range(base, CT):
         kept_v[s] = tt[spot(0, s), :T, :]
     keep = pltpu.make_async_copy(kept_v, kept, k_sem)
     keep.start()
-    relay(2)
-    relay(1)
 
     each_fill(lambda copy: copy.wait())
     keep.wait()
@@ -379,7 +402,7 @@
     CT = coarse_cols.shape[1]
     B = 3
     bf16, f32 = jnp.bfloat16, jnp.float32
-    smem = pl.BlockSpec(memory_space=pltpu.SMEM)
+    i32 = jnp.int32
     hbm = pl.BlockSpec(memory_space=pl.ANY)
     kept, got = pl.pallas_call(
         functools.partial(kernel, G, M),
@@ -387,7 +410,7 @@
             jax.ShapeDtypeStruct((CT, T, T), f32),
             jax.ShapeDtypeStruct((B - 1, CT, T, T), bf16),
         ),
-        in_specs=[smem] * 6 + [hbm] * 3,
+        in_specs=[hbm] * 9,
         out_specs=(hbm, hbm),
         scratch_shapes=[
             pltpu.VMEM((R, PT, T, T), bf16),
@@ -405,7 +428,14 @@
             pltpu.VMEM((B - 1, CT, T, T), bf16),
             pltpu.VMEM(((B - 1) * T, B * T), f32),
             pltpu.VMEM((CT, T, T), bf16),
-            pltpu.SemaphoreType.DMA,
+            pltpu.SMEM((D, R), i32),
+            pltpu.SMEM((O, R), i32),
+            pltpu.SMEM((R,), i32),
+            pltpu.SMEM((PT, R), i32),
+            pltpu.SMEM((1, S, send_rows.shape[1]), i32),
+            pltpu.SMEM((CT, coarse_cols.shape[0]), i32),
+            pltpu.SemaphoreType.DMA((6,)),
+            pltpu.SemaphoreType.DMA((CHUNKS,)),
             pltpu.SemaphoreType.DMA((CHUNKS,)),
             pltpu.SemaphoreType.DMA,
             pltpu.SemaphoreType.DMA((3,)),

time: 26.6 us -> 26.5 us (level)
  no operation moved by 1% of the time
where the time goes in v5:
time: 26.5 us; the launch traced here: 26.3 us
  Pallas kernels  24.3 us (92%)
  other arithmetic  2.06 us (8%)
    pallas_call x1, Pallas kernels, on_device(): pl.pallas_call(functools.partial(kernel, G, M), out_shape=(jax.ShapeDtype...  24.3 us
    broadcast_in_dim x1, other arithmetic, on_device(): return (kept + got[0].astype(f32) + got[1].astype(f32))[None]  2.06 us

profile of v5, /device:TPU:0, one launch (start us, length us, event | category | flops | bytes accessed | tf_op | source)
XLA Modules:
  0.0 26.3 jit_solution(7805956544980994322)
XLA Ops:
  0.0 24.3 %shard_map.91 = (f32[8,128,128]{2,1,0:T(8,128)}, bf16[2,8,128,128]{3,2,1,0:T(8,128)(2,1)}) custom-call(s32[4,16]{1,0:T(4,128)} %bitcast.14, s32[2,16]{1,0:T(2,128)} %bitcast.15, s32[16]{0:T(128)} %ocount_hbm.1, s32[2,16]{1,0:T(2,128)} %bitcast.16, s32[1,1,8]{2,1,0:T(1,128)} %bitcast.17, s32[8,32]{1,0:T(8,128)} %bitcast.13, bf16[16,2,128,128]{3,2,1,0:T(8,128)(2,1)} %p_hbm.1, ...), custom_call_target="tpu_custom_call" | custom-call | tf_op jit(solution)/shard_map/pallas_call | solution.py:407
  24.3 2.1 %fusion = f32[1,8,128,128]{3,2,1,0:T(8,128)} fusion(f32[8,128,128]{2,1,0:T(8,128)} %get-tuple-element.7, bf16[2,8,128,128]{3,2,1,0:T(8,128)(2,1)} %get-tuple-element.8), kind=kLoop, calls=%fused_computation.1 | loop fusion | flops 524288 | bytes 1572864 | tf_op jit(solution)/shard_map/broadcast_in_dim | solution.py:463

commit v6 on v5

--- a/solution.py
+++ b/solution.py
@@ -125,16 +125,14 @@
                 for lo, n in gap:
                     act(fill(b, lo, n))
 
+            some()
             if not relays:
-                some()
                 continue
-            fed = (relays[b] + hoff[b]) % G
             other = B - b
-            pl.when(jnp.logical_and(g != (relays[other] + hoff[other]) % G, g != fed))(some)
-
-            @pl.when(g == fed)
+
+            @pl.when(g == (relays[b] + hoff[b]) % G)
             def _(other=other):
-                act(fill(other, 0, CT))
+                act(fill(other, base, CT - base))
 
     zeros[...] = jnp.zeros((CT, T, T), bf16)
     each_fill(lambda copy: copy.start())
@@ -203,15 +201,12 @@
     }
     half = (CT - base) // 2
     rest = [(base, half), (base + half, CT - base - half)]
-    full = {b: spans[b][0] + spans[b][1] + rest for b in range(1, B)}
-    alone = {b: runs(set(range(base)) - set(sent[B - b])) for b in relays}
-
     def each_send(b, which, act):
         def direct():
             for lo, n in which:
                 act(group_copy(b, lo, n))
 
-        if not relays:
+        if not relays or which is not rest:
             direct()
             return
         pl.when(jnp.logical_and(g != feeds[b], g != relays[b]))(direct)
@@ -224,31 +219,20 @@
     def start(b, which):
         each_send(b, which, lambda copy: copy.start())
 
-    def add_and_send(b, lo, n, come):
-        if come:
-            feed_copy(B - b, lo, n).wait_recv()
+    def add_and_send(b, lo, n):
+        feed_copy(B - b, lo, n).wait_recv()
         for s in range(lo, lo + n):
-            total = None
-            if s >= base:
-                total = tt[spot(b, s), b * T : (b + 1) * T, :]
-            elif s in sent[b]:
-                total = loc[(b - 1) * T : b * T, sent[b][s] * T : (sent[b][s] + 1) * T]
-            if come:
-                term = fed_v[s].astype(f32)
-                total = term if total is None else total + term
+            total = tt[spot(b, s), b * T : (b + 1) * T, :] + fed_v[s].astype(f32)
             gs[b - 1, s] = total.astype(bf16)
         group_copy(b, lo, n).start()
 
-    def relay(part):
+    def relay():
         for b in relays:
 
             @pl.when(g == relays[b])
             def _(b=b):
-                for lo, n in rest if part == 2 else spans[B - b][part]:
-                    add_and_send(b, lo, n, True)
-                if part == 1:
-                    for lo, n in alone[b]:
-                        add_and_send(b, lo, n, False)
+                for lo, n in rest:
+                    add_and_send(b, lo, n)
 
     def local_part(part):
         at = slice(cols[part][0] * T, (cols[part][-1] + 1) * T)
@@ -311,8 +295,9 @@
         return at
 
     local_part(0)
-    stage(1, 0)
-    start(1, spans[1][0])
+    for b in (1, 2):
+        stage(b, 0)
+        start(b, spans[b][0])
 
     o_copy.wait()
     for f in range(R):
@@ -324,8 +309,6 @@
                 block = term if block is None else block + term
             ar[f * T : (f + 1) * T, r * T : (r + 1) * T] = block
     mid = remote_mid(T, B * T)
-    stage(2, 0)
-    start(2, spans[2][0])
 
     tt[3 * B] = jnp.zeros(tt.shape[1:], f32)
     remote(mid, T, B * T, True)
@@ -338,7 +321,6 @@
     start(2, rest)
     stage(2, 1)
     start(2, spans[2][1])
-    relay(0)
 
     local = jnp.dot(pmt[:T, :], x[...], preferred_element_type=f32)
     for s in range(base):
@@ -347,8 +329,7 @@
             kept_v[s] = local[:, b2 * T : (b2 + 1) * T]
         else:
             kept_v[s] = jnp.zeros((T, T), f32)
-    relay(2)
-    relay(1)
+    relay()
     remote(remote_mid(0, T), 0, T, False)
     for s in range(base, CT):
         kept_v[s] = tt[spot(0, s), :T, :]
@@ -360,27 +341,26 @@
     for copy in m_copies:
         copy.wait_send()
     for b in range(1, B):
-        each_send(b, full[b], lambda copy: copy.wait_send())
+        for which in spans[b] + [rest]:
+            each_send(b, which, lambda copy: copy.wait_send())
+        for lo, n in spans[b][0] + spans[b][1]:
+            group_copy(b, lo, n).wait_recv()
+
+        def last(b=b):
+            for lo, n in rest:
+                group_copy(b, lo, n).wait_recv()
+
         if not relays:
-            for lo, n in full[b]:
-                group_copy(b, lo, n).wait_recv()
+            last()
             continue
-        whole = spans[B - b][0] + spans[B - b][1] + alone[b] + rest
 
         @pl.when(g == relays[b])
-        def _(b=b, whole=whole):
-            for lo, n in whole:
+        def _(b=b):
+            for lo, n in rest:
                 group_copy(b, lo, n).wait_send()
 
-        @pl.when(g == (relays[b] + hoff[b]) % G)
-        def _(b=b, whole=whole):
-            for lo, n in whole:
-                group_copy(b, lo, n).wait_recv()
-
-        @pl.when(lax.rem(g, 2) == 1)
-        def _(b=b):
-            for lo, n in full[b]:
-                group_copy(b, lo, n).wait_recv()
+        to = (relays[b] + hoff[b]) % G
+        pl.when(jnp.logical_or(g == to, lax.rem(g, 2) == 1))(last)
 
 
 def on_device(

time: 26.5 us -> 25.3 us (0.955)
  Pallas kernels: 24.3 us -> 23.1 us
    pallas_call x1, Pallas kernels: 24.3 us -> 23.1 us  [on_device(): pl.pallas_call(functools.partial(kernel, G, M), out_shape=(jax.ShapeDtype...]
where the time goes in v6:
time: 25.3 us; the launch traced here: 25.2 us
  Pallas kernels  23.1 us (91%)
  other arithmetic  2.06 us (8%)
    pallas_call x1, Pallas kernels, on_device(): pl.pallas_call(functools.partial(kernel, G, M), out_shape=(jax.ShapeDtype...  23.1 us
    broadcast_in_dim x1, other arithmetic, on_device(): return (kept + got[0].astype(f32) + got[1].astype(f32))[None]  2.06 us

profile of v6, /device:TPU:0, one launch (start us, length us, event | category | flops | bytes accessed | tf_op | source)
XLA Modules:
  0.0 25.2 jit_solution(16649440730719010311)
XLA Ops:
  0.0 23.1 %shard_map.91 = (f32[8,128,128]{2,1,0:T(8,128)}, bf16[2,8,128,128]{3,2,1,0:T(8,128)(2,1)}) custom-call(s32[4,16]{1,0:T(4,128)} %bitcast.14, s32[2,16]{1,0:T(2,128)} %bitcast.15, s32[16]{0:T(128)} %ocount_hbm.1, s32[2,16]{1,0:T(2,128)} %bitcast.16, s32[1,1,8]{2,1,0:T(1,128)} %bitcast.17, s32[8,32]{1,0:T(8,128)} %bitcast.13, bf16[16,2,128,128]{3,2,1,0:T(8,128)(2,1)} %p_hbm.1, ...), custom_call_target="tpu_custom_call" | custom-call | tf_op jit(solution)/shard_map/pallas_call | solution.py:387
  23.1 2.1 %fusion = f32[1,8,128,128]{3,2,1,0:T(8,128)} fusion(f32[8,128,128]{2,1,0:T(8,128)} %get-tuple-element.7, bf16[2,8,128,128]{3,2,1,0:T(8,128)(2,1)} %get-tuple-element.8), kind=kLoop, calls=%fused_computation.1 | loop fusion | flops 524288 | bytes 1572864 | tf_op jit(solution)/shard_map/broadcast_in_dim | solution.py:443

commit v7 on v6

--- a/solution.py
+++ b/solution.py
@@ -199,8 +199,8 @@
         b: [runs(s for s, b2 in sent[b].items() if b2 in part) for part in cols]
         for b in range(1, B)
     }
-    half = (CT - base) // 2
-    rest = [(base, half), (base + half, CT - base - half)]
+    rest = [(s, 1) for s in range(base, CT)]
+
     def each_send(b, which, act):
         def direct():
             for lo, n in which:
@@ -218,6 +218,24 @@
 
     def start(b, which):
         each_send(b, which, lambda copy: copy.start())
+
+    def start_feeds():
+        for b in relays:
+
+            @pl.when(g == feeds[b])
+            def _(b=b):
+                for lo, n in rest:
+                    feed_copy(b, lo, n).start()
+
+    def start_rest(b):
+        def direct():
+            for lo, n in rest:
+                group_copy(b, lo, n).start()
+
+        if relays:
+            pl.when(jnp.logical_and(g != feeds[b], g != relays[b]))(direct)
+        else:
+            direct()
 
     def add_and_send(b, lo, n):
         feed_copy(B - b, lo, n).wait_recv()
@@ -313,14 +331,14 @@
     tt[3 * B] = jnp.zeros(tt.shape[1:], f32)
     remote(mid, T, B * T, True)
     stage_rest(1)
-    start(1, rest)
+    stage_rest(2)
+    start_feeds()
     local_part(1)
-    stage(1, 1)
-    start(1, spans[1][1])
-    stage_rest(2)
-    start(2, rest)
-    stage(2, 1)
-    start(2, spans[2][1])
+    for b in (1, 2):
+        stage(b, 1)
+        start(b, spans[b][1])
+    for b in (1, 2):
+        start_rest(b)
 
     local = jnp.dot(pmt[:T, :], x[...], preferred_element_type=f32)
     for s in range(base):

time: 25.3 us -> 25.4 us (level)
  no operation moved by 1% of the time
where the time goes in v7:
time: 25.4 us; the launch traced here: 25.2 us
  Pallas kernels  23.1 us (91%)
  other arithmetic  2.06 us (8%)
    pallas_call x1, Pallas kernels, on_device(): pl.pallas_call(functools.partial(kernel, G, M), out_shape=(jax.ShapeDtype...  23.1 us
    broadcast_in_dim x1, other arithmetic, on_device(): return (kept + got[0].astype(f32) + got[1].astype(f32))[None]  2.06 us

profile of v7, /device:TPU:0, one launch (start us, length us, event | category | flops | bytes accessed | tf_op | source)
XLA Modules:
  0.0 25.2 jit_solution(7845491930940033295)
XLA Ops:
  0.0 23.1 %shard_map.91 = (f32[8,128,128]{2,1,0:T(8,128)}, bf16[2,8,128,128]{3,2,1,0:T(8,128)(2,1)}) custom-call(s32[4,16]{1,0:T(4,128)} %bitcast.14, s32[2,16]{1,0:T(2,128)} %bitcast.15, s32[16]{0:T(128)} %ocount_hbm.1, s32[2,16]{1,0:T(2,128)} %bitcast.16, s32[1,1,8]{2,1,0:T(1,128)} %bitcast.17, s32[8,32]{1,0:T(8,128)} %bitcast.13, bf16[16,2,128,128]{3,2,1,0:T(8,128)(2,1)} %p_hbm.1, ...), custom_call_target="tpu_custom_call" | custom-call | tf_op jit(solution)/shard_map/pallas_call | solution.py:405
  23.1 2.1 %fusion = f32[1,8,128,128]{3,2,1,0:T(8,128)} fusion(f32[8,128,128]{2,1,0:T(8,128)} %get-tuple-element.7, bf16[2,8,128,128]{3,2,1,0:T(8,128)(2,1)} %get-tuple-element.8), kind=kLoop, calls=%fused_computation.1 | loop fusion | flops 524288 | bytes 1572864 | tf_op jit(solution)/shard_map/broadcast_in_dim | solution.py:461

commit v8 on v7

--- a/solution.py
+++ b/solution.py
@@ -340,6 +340,8 @@
     for b in (1, 2):
         start_rest(b)
 
+    relay()
+
     local = jnp.dot(pmt[:T, :], x[...], preferred_element_type=f32)
     for s in range(base):
         if s in sent[0]:
@@ -347,7 +349,6 @@
             kept_v[s] = local[:, b2 * T : (b2 + 1) * T]
         else:
             kept_v[s] = jnp.zeros((T, T), f32)
-    relay()
     remote(remote_mid(0, T), 0, T, False)
     for s in range(base, CT):
         kept_v[s] = tt[spot(0, s), :T, :]

time: 25.4 us -> 25.4 us (level)
  no operation moved by 1% of the time
where the time goes in v8:
time: 25.4 us; the launch traced here: 25.2 us
  Pallas kernels  23.1 us (91%)
  other arithmetic  2.06 us (8%)
    pallas_call x1, Pallas kernels, on_device(): pl.pallas_call(functools.partial(kernel, G, M), out_shape=(jax.ShapeDtype...  23.1 us
    broadcast_in_dim x1, other arithmetic, on_device(): return (kept + got[0].astype(f32) + got[1].astype(f32))[None]  2.06 us

profile of v8, /device:TPU:0, one launch (start us, length us, event | category | flops | bytes accessed | tf_op | source)
XLA Modules:
  0.0 25.2 jit_solution(1285065250013010874)
XLA Ops:
  0.0 23.1 %shard_map.91 = (f32[8,128,128]{2,1,0:T(8,128)}, bf16[2,8,128,128]{3,2,1,0:T(8,128)(2,1)}) custom-call(s32[4,16]{1,0:T(4,128)} %bitcast.14, s32[2,16]{1,0:T(2,128)} %bitcast.15, s32[16]{0:T(128)} %ocount_hbm.1, s32[2,16]{1,0:T(2,128)} %bitcast.16, s32[1,1,8]{2,1,0:T(1,128)} %bitcast.17, s32[8,32]{1,0:T(8,128)} %bitcast.13, bf16[16,2,128,128]{3,2,1,0:T(8,128)(2,1)} %p_hbm.1, ...), custom_call_target="tpu_custom_call" | custom-call | tf_op jit(solution)/shard_map/pallas_call | solution.py:406
  23.1 2.1 %fusion = f32[1,8,128,128]{3,2,1,0:T(8,128)} fusion(f32[8,128,128]{2,1,0:T(8,128)} %get-tuple-element.7, bf16[2,8,128,128]{3,2,1,0:T(8,128)(2,1)} %get-tuple-element.8), kind=kLoop, calls=%fused_computation.1 | loop fusion | flops 524288 | bytes 1572864 | tf_op jit(solution)/shard_map/broadcast_in_dim | solution.py:462
